TPU v7x, 128 devices: a whole 4x4x4 slice. The times are simulated.
128 devices in a mesh: row: 8 (over x, y_lo), col: 16 (over z, y_hi, core).
Axes of the slice: x: 4, y: 4 (y_hi: 2, y_lo: 2; y = y_hi * 2 + y_lo), z: 4, core: 2. Of those that a mesh axis runs over, the one named last changes fastest.
Arguments:
- pair: bfloat16 [512, 512, 128], P('row', 'col'), may hold values from -6 to 6
- gain_one: bfloat16 [128], replicated, may hold values from 0.25 to 1.75
- proj_one: bfloat16 [128, 512], replicated, may hold values from -0.5 to 0.5
- bias_one: bfloat16 [128, 4], replicated, may hold values from -6 to 6
- out_one: bfloat16 [128, 128], replicated, may hold values from -0.5 to 0.5
- gain_two: bfloat16 [128], replicated, may hold values from 0.25 to 1.75
- proj_two: bfloat16 [128, 512], replicated, may hold values from -0.5 to 0.5
- bias_two: bfloat16 [128, 4], replicated, may hold values from -6 to 6
- out_two: bfloat16 [128, 128], replicated, may hold values from -0.5 to 0.5
Outputs:
- pair_out: bfloat16 [512, 512, 128], P('row', 'col')
All inputs are finite; a program needn't handle non-finite values.
Results may differ from a plain program's by a relative error of at most 0.03.
Values may be sent and summed in bfloat16 or wider, within the bound.
A program may use at most 128 MiB of HBM per device.

v0:
```python
import jax
import jax.numpy as jnp
from jax import lax
from jax.sharding import PartitionSpec as P

C = 128
H = 4
DH = 32


def normalize(pair, gain):
    values = pair.astype(jnp.float32)
    mean = jnp.mean(values, axis=-1, keepdims=True)
    spread = jnp.mean((values - mean) ** 2, axis=-1, keepdims=True)
    return ((values - mean) * lax.rsqrt(spread + 1e-05) * gain.astype(jnp.float32)).astype(
        jnp.bfloat16
    )


def linear(inputs, weight):
    flat = inputs.reshape(-1, inputs.shape[-1])
    result = jnp.dot(flat, weight, preferred_element_type=jnp.float32)
    return result.reshape(inputs.shape[:-1] + (weight.shape[1],))


def full_bias(normed, bias_weight):
    local_bias = jnp.transpose(linear(normed, bias_weight).astype(jnp.bfloat16), (2, 0, 1))
    banded = lax.all_gather(local_bias, "col", axis=2, tiled=True)
    return lax.all_gather(banded, "row", axis=1, tiled=True)


def local_parts(normed, proj):
    query = (linear(normed, proj[:, 0:C]) * DH ** (-0.5)).astype(jnp.bfloat16)
    gate = jax.nn.sigmoid(linear(normed, proj[:, 3 * C : 4 * C]))
    return (query, gate)


def key_parts(normed, proj):
    keyval = linear(normed, proj[:, C : 3 * C]).astype(jnp.bfloat16)
    return (keyval[..., :C], keyval[..., C:])


def body(pair, gain_one, proj_one, bias_one, out_one, gain_two, proj_two, bias_two, out_two):
    rows_here = pair.shape[0]
    cols_here = pair.shape[1]
    normed = normalize(pair, gain_one)
    whole_bias = full_bias(normed, bias_one)
    first_col = lax.axis_index("col") * cols_here
    band_bias = lax.dynamic_slice_in_dim(whole_bias, first_col, cols_here, 1)
    query, gate = local_parts(normed, proj_one)
    keys, values = key_parts(normed, proj_one)
    keys, values = (
        lax.all_gather(keys, "col", axis=1, tiled=True),
        lax.all_gather(values, "col", axis=1, tiled=True),
    )
    total = keys.shape[1]
    query_heads = query.reshape(rows_here, cols_here, H, DH)
    key_heads = keys.reshape(rows_here, total, H, DH)
    value_heads = values.reshape(rows_here, total, H, DH)
    score = jnp.einsum(
        "ijhd,ikhd->hijk", query_heads, key_heads, preferred_element_type=jnp.float32
    )
    score = score + band_bias[:, None, :, :].astype(jnp.float32)
    prob = jax.nn.softmax(score, axis=-1).astype(jnp.bfloat16)
    attn = jnp.einsum("hijk,ikhd->ijhd", prob, value_heads, preferred_element_type=jnp.float32)
    gated = (gate * attn.reshape(rows_here, cols_here, C)).astype(jnp.bfloat16)
    middle = (pair.astype(jnp.float32) + linear(gated, out_one)).astype(jnp.bfloat16)
    normed = normalize(middle, gain_two)
    whole_bias = full_bias(normed, bias_two)
    first_row = lax.axis_index("row") * rows_here
    strip_bias = jnp.transpose(
        lax.dynamic_slice_in_dim(whole_bias, first_row, rows_here, 2), (0, 2, 1)
    )
    query, gate = local_parts(normed, proj_two)
    keys, values = key_parts(normed, proj_two)
    keys, values = (
        lax.all_gather(keys, "row", axis=0, tiled=True),
        lax.all_gather(values, "row", axis=0, tiled=True),
    )
    total = keys.shape[0]
    query_heads = query.reshape(rows_here, cols_here, H, DH)
    key_heads = keys.reshape(total, cols_here, H, DH)
    value_heads = values.reshape(total, cols_here, H, DH)
    score = jnp.einsum(
        "ijhd,kjhd->hijk", query_heads, key_heads, preferred_element_type=jnp.float32
    )
    score = score + strip_bias[:, :, None, :].astype(jnp.float32)
    prob = jax.nn.softmax(score, axis=-1).astype(jnp.bfloat16)
    attn = jnp.einsum("hijk,kjhd->ijhd", prob, value_heads, preferred_element_type=jnp.float32)
    gated = (gate * attn.reshape(rows_here, cols_here, C)).astype(jnp.bfloat16)
    return (middle.astype(jnp.float32) + linear(gated, out_two)).astype(jnp.bfloat16)


def solution(mesh):
    in_specs = (P("row", "col", None), P(), P(), P(), P(), P(), P(), P(), P())
    out_specs = P("row", "col", None)
    return jax.shard_map(body, mesh=mesh, in_specs=in_specs, out_specs=out_specs, check_vma=False)
```

profile of v0, /device:TPU:9, one launch (start us, length us, event | category | flops | bytes accessed | tf_op | source)
XLA Modules:
  0.0 559.6 jit_solution(2386081853709472694)
XLA Ops:
  10.4 1.9 fusion.34
  12.4 27.5 %all_gather.26 = bf16[4,64,512]{1,0,2:T(4,128)(2,1)S(1)} all-gather(bf16[4,64,32]{1,0,2:T(4,128)(2,1)S(1)} %copy.84), channel_id=1, replica_groups=mesh['row'=8,'col'=16] {'col'}, dimensions={2}, use_global_device_ids=true | all-gather | bytes 278528 | tf_op jit(solution)/shard_map/all_gather | solution.py:28
  41.1 1.8 convolution_convert_fusion.1
  47.7 4.0 copy.82
  51.7 36.8 %all-gather.11.cloned.1.call-done = bf16[4,512,512]{2,0,1:T(4,128)(2,1)} async-done(((bf16[4,64,512]{2,0,1:T(4,128)(2,1)}), bf16[4,512,512]{2,0,1:T(4,128)(2,1)}) %all-gather.11.cloned.1.call-update) | async-done | bytes 2097168 | tf_op jit(solution)/shard_map/all_gather | solution.py:29
  89.5 79.0 %all-gather.9.cloned.1.call-done = bf16[64,512,128]{2,1,0:T(8,128)(2,1)} async-done(((bf16[64,32,128]{2,1,0:T(8,128)(2,1)}), bf16[64,512,128]{2,1,0:T(8,128)(2,1)}) %all-gather.9.cloned.1.call-update) | async-done | bytes 8388624 | tf_op jit(solution)/shard_map/all_gather | solution.py:53
  168.5 11.9 %copy.81 = bf16[64,512,128]{1,2,0:T(8,128)(2,1)} copy(bf16[64,512,128]{2,1,0:T(8,128)(2,1)} %all-gather.9.cloned.1.call-done) | data formatting | bytes 16777216 | tf_op jit(solution)/shard_map/all_gather | solution.py:53
  180.4 11.5 %fusion.10 = f32[4,64,32,512]{3,2,1,0:T(8,128)} fusion(bf16[64,32,4,32]{3,1,0,2:T(8,128)(2,1)S(1)} %copy.82, bf16[64,512,4,32]{1,3,2,0:T(8,128)(2,1)} %bitcast.68), kind=kOutput, calls=%fused_computation.14 | convolution fusion | flops 268435456 | bytes 25690112 | tf_op jit(solution)/shard_map/ijhd,ikhd->hijk/dot_general | solution.py:60
  191.9 18.6 %fusion.79 = (f32[4,64,32]{2,1,0:T(8,128)S(1)}, f32[4,64,32,512]{3,2,1,0:T(8,128)}) fusion(f32[4,64,32,512]{3,2,1,0:T(8,128)} %fusion.10, f32[4,32,512]{2,1,0:T(8,128)S(1)} %copy_convert_fusion), kind=kOutput, calls=%fused_computation.90 | output fusion | flops 16777728 | bytes 33849344 | tf_op jit(solution)/shard_map/sub | solution.py:64
  210.5 35.0 %all-gather.7.cloned.1.call-done = bf16[64,512,128]{2,1,0:T(8,128)(2,1)} async-done(((bf16[64,32,128]{2,1,0:T(8,128)(2,1)}), bf16[64,512,128]{2,1,0:T(8,128)(2,1)}) %all-gather.7.cloned.1.call-update) | async-done | bytes 8388624 | tf_op jit(solution)/shard_map/all_gather | solution.py:54
  245.5 12.0 %copy.79 = bf16[64,512,128]{1,2,0:T(8,128)(2,1)} copy(bf16[64,512,128]{2,1,0:T(8,128)(2,1)} %all-gather.7.cloned.1.call-done) | data formatting | bytes 16777216 | tf_op jit(solution)/shard_map/all_gather | solution.py:54
  257.5 11.7 %fusion.8 = f32[64,4,32,32]{3,2,1,0:T(8,128)} fusion(bf16[64,512,4,32]{1,3,2,0:T(8,128)(2,1)} %bitcast.70, f32[4,64,32,512]{3,2,1,0:T(8,128)} %get-tuple-element.10, f32[4,64,32]{2,1,0:T(8,128)S(1)} %get-tuple-element.9), kind=kOutput, calls=%fused_computation.12 | convolution fusion | flops 276824064 | bytes 26247168 | tf_op jit(solution)/shard_map/hijk,ikhd->ijhd/dot_general | solution.py:65
  269.1 2.9 copy.89
  274.7 23.0 %all_gather.30 = bf16[4,64,512]{1,0,2:T(4,128)(2,1)S(1)} all-gather(bf16[4,64,32]{1,0,2:T(4,128)(2,1)S(1)} %copy.95), channel_id=1, replica_groups=mesh['row'=8,'col'=16] {'col'}, dimensions={2}, use_global_device_ids=true | all-gather | bytes 278528 | tf_op jit(solution)/shard_map/all_gather | solution.py:28
  303.2 44.6 %all-gather.17.cloned.1.call-done = bf16[4,512,512]{2,0,1:T(4,128)(2,1)} async-done(((bf16[4,64,512]{2,0,1:T(4,128)(2,1)}), bf16[4,512,512]{2,0,1:T(4,128)(2,1)}) %all-gather.17.cloned.1.call-update) | async-done | bytes 2097168 | tf_op jit(solution)/shard_map/all_gather | solution.py:29
  349.6 88.8 %all-gather.15.cloned.1.call-done = bf16[512,32,128]{2,1,0:T(8,128)(2,1)} async-done(((bf16[64,32,128]{2,1,0:T(8,128)(2,1)}), bf16[512,32,128]{2,1,0:T(8,128)(2,1)}) %all-gather.15.cloned.1.call-update) | async-done | bytes 4194320 | tf_op jit(solution)/shard_map/all_gather | solution.py:77
  438.4 7.6 %copy.91 = bf16[512,32,128]{0,2,1:T(8,128)(2,1)} copy(bf16[512,32,128]{2,1,0:T(8,128)(2,1)} %all-gather.15.cloned.1.call-done) | data formatting | bytes 8388608 | tf_op jit(solution)/shard_map/all_gather | solution.py:77
  446.0 10.3 %fusion.14 = f32[4,32,512,64]{2,3,1,0:T(8,128)} fusion(bf16[512,32,4,32]{0,3,2,1:T(8,128)(2,1)} %bitcast.69, bf16[64,32,4,32]{0,3,2,1:T(8,128)(2,1)S(1)} %bitcast.71), kind=kOutput, calls=%fused_computation.18 | convolution fusion | flops 268435456 | bytes 21495808 | tf_op jit(solution)/shard_map/ijhd,kjhd->hijk/dot_general | solution.py:84
  456.3 17.6 %fusion.84 = (f32[4,64,32]{1,2,0:T(8,128)S(1)}, f32[4,64,32,512]{3,1,2,0:T(8,128)}) fusion(f32[4,32,512,64]{2,3,1,0:T(8,128)} %fusion.14, f32[4,64,512]{2,1,0:T(8,128)S(1)} %copy.97), kind=kOutput, calls=%fused_computation.91 | output fusion | flops 16777728 | bytes 34111488 | tf_op jit(solution)/shard_map/sub | solution.py:88
  473.9 58.3 %all-gather.13.cloned.1.call-done = bf16[512,32,128]{2,1,0:T(8,128)(2,1)} async-done(((bf16[64,32,128]{2,1,0:T(8,128)(2,1)}), bf16[512,32,128]{2,1,0:T(8,128)(2,1)}) %all-gather.13.cloned.1.call-update) | async-done | bytes 4194320 | tf_op jit(solution)/shard_map/all_gather | solution.py:78
  532.2 7.6 %copy.90 = bf16[512,32,128]{0,2,1:T(8,128)(2,1)} copy(bf16[512,32,128]{2,1,0:T(8,128)(2,1)} %all-gather.13.cloned.1.call-done) | data formatting | bytes 8388608 | tf_op jit(solution)/shard_map/all_gather | solution.py:78
  539.7 8.3 %fusion.6 = f32[32,4,32,64]{3,2,1,0:T(8,128)S(1)} fusion(bf16[512,32,4,32]{0,3,2,1:T(8,128)(2,1)} %bitcast.74, f32[4,64,32,512]{3,1,2,0:T(8,128)} %get-tuple-element.14, f32[4,64,32]{1,2,0:T(8,128)S(1)} %get-tuple-element.13), kind=kOutput, calls=%fused_computation.10 | convolution fusion | flops 276824064 | bytes 22052864 | tf_op jit(solution)/shard_map/hijk,kjhd->ijhd/dot_general | solution.py:89
  548.1 1.8 copy.99
  549.8 2.9 fusion.27
  (54 shorter events, 20.6 us)
Async XLA Ops:
  6.5 265.5 %copy-start = (bf16[128,128]{1,0:T(8,128)(2,1)S(1)}, bf16[128,128]{1,0:T(8,128)(2,1)}, u32[]{:S(2)}) copy-start(bf16[128,128]{1,0:T(8,128)(2,1)} %param.13) | copy-start | bytes 98308
  6.5 38.5 %copy-start.2 = (bf16[64,32,128]{2,1,0:T(8,128)(2,1)S(1)}, bf16[64,32,128]{2,1,0:T(8,128)(2,1)}, u32[]{:S(2)}) copy-start(bf16[64,32,128]{2,1,0:T(8,128)(2,1)} %param.9) | copy-start | bytes 1572868
  6.5 38.5 %copy-start.3 = (bf16[128,512]{1,0:T(8,128)(2,1)S(1)}, bf16[128,512]{1,0:T(8,128)(2,1)}, u32[]{:S(2)}) copy-start(bf16[128,512]{1,0:T(8,128)(2,1)} %param.11) | copy-start | bytes 393220
  6.5 45.2 %copy-start.7 = (bf16[128]{0:T(256)(128)(2,1)S(1)}, bf16[128]{0:T(256)(128)(2,1)}, u32[]{:S(2)}) copy-start(bf16[128]{0:T(256)(128)(2,1)} %param.14) | copy-start | bytes 772
  6.5 82.0 %all-gather.11.cloned.1.call-start = ((), (), s32[]{:S(2)}) async-start(), calls=%async_computation.2 | async-start | bytes 2359296 | tf_op jit(solution)/shard_map/all_gather | solution.py:29
  41.1 127.4 %all-gather.9.cloned.1.call-start = ((), (), s32[]{:S(2)}) async-start(), calls=%async_computation.1 | async-start | bytes 8912896 | tf_op jit(solution)/shard_map/all_gather | solution.py:53
  44.1 201.4 %all-gather.7.cloned.1.call-start = ((), (), s32[]{:S(2)}) async-start(), calls=%async_computation | async-start | bytes 8912896 | tf_op jit(solution)/shard_map/all_gather | solution.py:54
  44.8 303.0 %all-gather.17.cloned.1.call-start = ((), (), s32[]{:S(2)}) async-start(), calls=%async_computation.5 | async-start | bytes 2359296 | tf_op jit(solution)/shard_map/all_gather | solution.py:29
  269.1 4.5 copy-start.6
  269.1 29.7 %copy-start.4 = (bf16[128,512]{1,0:T(8,128)(2,1)S(1)}, bf16[128,512]{1,0:T(8,128)(2,1)}, u32[]{:S(2)}) copy-start(bf16[128,512]{1,0:T(8,128)(2,1)} %param.15) | copy-start | bytes 393220
  298.7 139.6 %all-gather.15.cloned.1.call-start = ((), (), s32[]{:S(2)}) async-start(), calls=%async_computation.4 | async-start | bytes 4718592 | tf_op jit(solution)/shard_map/all_gather | solution.py:77
  301.0 231.2 %all-gather.13.cloned.1.call-start = ((), (), s32[]{:S(2)}) async-start(), calls=%async_computation.3 | async-start | bytes 4718592 | tf_op jit(solution)/shard_map/all_gather | solution.py:78
  539.7 10.1 %copy-start.5 = (bf16[128,128]{1,0:T(8,128)(2,1)S(1)}, bf16[128,128]{1,0:T(8,128)(2,1)}, u32[]{:S(2)}) copy-start(bf16[128,128]{1,0:T(8,128)(2,1)} %param.17) | copy-start | bytes 98308
  539.7 13.0 %copy-start.1 = (bf16[128,128]{1,0:T(8,128)(2,1)S(1)}, bf16[128,128]{1,0:T(8,128)(2,1)}, u32[]{:S(2)}) copy-start(bf16[128,128]{1,0:T(8,128)(2,1)} %param.13) | copy-start | bytes 98308
Sparse Core Ops, SparseCore 0:
  41.2 47.2 all-gather.10
  90.9 77.5 all-gather.8
  170.8 74.6 all-gather.6
  298.9 48.9 all-gather.16
  349.3 89.0 all-gather.14
  439.9 92.2 all-gather.12
where the time goes:
time: 564 us; the launch traced here: 560 us
  waiting for transfers between devices  344 us (61%)
  local copies, waits for them, and re-layouts  56.1 us (10%)
  matrix products  53 us (9%)
  blocking collectives  50.5 us (9%)
  other arithmetic  42.1 us (7%)
  between operations  13.7 us (2%)
    all_gather x1, waiting for transfers between devices, body(): lax.all_gather(keys, 'row', axis=0, tiled=True)  88.8 us
    all_gather x2, waiting for transfers between devices, full_bias(): return lax.all_gather(banded, 'row', axis=1, tiled=True)  81.4 us
    all_gather x1, waiting for transfers between devices, body(): lax.all_gather(keys, 'col', axis=1, tiled=True)  79 us
    all_gather x1, waiting for transfers between devices, body(): lax.all_gather(values, 'row', axis=0, tiled=True)  58.3 us
    all_gather x2, blocking collectives, full_bias(): banded = lax.all_gather(local_bias, 'col', axis=2, tiled=True)  50.5 us
    sub x2, other arithmetic, body(): prob = jax.nn.softmax(score, axis=-1).astype(jnp.bfloat16)  36.3 us
    all_gather x1, waiting for transfers between devices, body(): lax.all_gather(values, 'col', axis=1, tiled=True)  35 us
    all_gather x1, local copies, waits for them, and re-layouts, body(): lax.all_gather(values, 'col', axis=1, tiled=True)  12 us
  transfers between devices with their start and end apart: 6, of which 6 were waited for; matrix products, arithmetic and copies ran while one was open for 17% of the time, Pallas kernels for 0%

commit v1 on v0

v1 whole, which is shorter than its diff:
```python
import jax
import jax.numpy as jnp
from jax import lax
from jax.experimental import pallas as pl
from jax.experimental.pallas import tpu as pltpu
from jax.sharding import PartitionSpec as P

C = 128
H = 4
DH = 32
N = 512
ROWS = 8
COLS = 16
DEVS = ROWS * COLS
OWN = N // DEVS
ROWS_HERE = N // ROWS
COLS_HERE = N // COLS
BLOCKS = 4
LANES = N // BLOCKS
CHUNK = 64
ONES = 16
LOG2E = 1.4426950408889634
MESH = pl.DeviceIdType.MESH
F32 = jnp.float32
BF16 = jnp.bfloat16
VMEM = pl.BlockSpec(memory_space=pltpu.VMEM)


def layer_norm(values, gain):
    mean = jnp.mean(values, axis=-1, keepdims=True)
    centred = values - mean
    spread = jnp.mean(centred * centred, axis=-1, keepdims=True)
    return centred * lax.rsqrt(spread + 1e-05) * gain


def dot(left, right):
    return jnp.dot(left, right, preferred_element_type=F32)


def dot_nt(left, right):
    return lax.dot_general(left, right, (((1,), (1,)), ((), ())), preferred_element_type=F32)


def device_of(x, y, z, core):
    x, y, z, core = lax.rem(x, 4), lax.rem(y, 4), lax.rem(z, 4), lax.rem(core, 2)
    return (x * 2 + lax.rem(y, 2), (z * 2 + y // 2) * 2 + core)


def remote(src, dst, send_sem, recv_sem, target):
    return pltpu.make_async_remote_copy(
        src_ref=src, dst_ref=dst, send_sem=send_sem, recv_sem=recv_sem,
        device_id=target, device_id_type=MESH,
    )


def kernel(
    pair_ref, gain_one_ref, proj_one_ref, bias_one_ref, out_one_ref,
    gain_two_ref, proj_two_ref, bias_two_ref, out_two_ref, block_ref,
    rows, whole_one, whole_two, tiles, columns, result, landed,
    flat_f, chunk_f, small_f, line_f, bias_f, values_f, query, keys, turned, gate_f, prob,
    own_sem, rows_send, rows_recv, plane_send, plane_recv, ring_send, ring_recv, pair_send, pair_recv,
    tile_send, tile_recv, plane2_send, plane2_recv, ring2_send, ring2_recv, pair2_send, pair2_recv,
    back_send, back_recv,
):
    row, col = lax.axis_index("row"), lax.axis_index("col")
    me = row * COLS + col
    x, z, core = row // 2, col // 4, lax.rem(col, 2)
    ylo, yhi = lax.rem(row, 2), lax.rem(col // 2, 2)
    y = 2 * yhi + ylo
    sibling = (row, col + 1 - 2 * core)

    barrier = pltpu.get_barrier_semaphore()

    @pl.loop(1, DEVS)
    def _(step):
        other = lax.rem(me + step, DEVS)
        pl.semaphore_signal(
            barrier, inc=1, device_id=(other // COLS, lax.rem(other, COLS)), device_id_type=MESH
        )

    gain_one = gain_one_ref[...].astype(F32)
    bias_one_t = jnp.transpose(bias_one_ref[...].astype(F32)).astype(BF16)

    @pl.loop(0, 8)
    def _(part):
        values = pair_ref[pl.ds(part * 8, 8)].reshape(256, C).astype(F32)
        flat_f[pl.ds(part * 256, 256), :] = layer_norm(values, gain_one)

    for k in range(16):
        both = jnp.concatenate(
            [flat_f[pl.ds(k, ROWS_HERE, COLS_HERE), :], flat_f[pl.ds(16 + k, ROWS_HERE, COLS_HERE), :]], axis=0
        ).astype(BF16)
        found = dot_nt(bias_one_t, both)
        for head in range(H):
            chunk_f[head * 16 + k, :] = found[head]
    whole_one[x, ylo, z, yhi, core] = chunk_f[...].astype(BF16)

    pl.semaphore_wait(barrier, DEVS - 1)

    def plane_copy(step):
        mine = whole_one.at[x, ylo, z, yhi, core]
        to = device_of(x, y + step // 4, z + lax.rem(step, 4), core)
        return remote(mine, mine, plane_send.at[step], plane_recv.at[step], to)

    def rows_copy(step):
        other = lax.rem(col + step, COLS)
        return remote(
            pair_ref.at[pl.ds(other * OWN, OWN)], rows.at[col], rows_send.at[step], rows_recv.at[step], (row, other)
        )

    def ring_copy(step):
        slab = whole_one.at[x, :, :, :, core]
        return remote(slab, slab, ring_send.at[step], ring_recv.at[step], device_of(x + step, y, z, core))

    def pair_copy(step, plane):
        slab = whole_one.at[plane, :, :, :, core]
        return remote(slab, slab, pair_send.at[step], pair_recv.at[step], sibling)

    @pl.loop(1, 16)
    def _(step):
        plane_copy(step).start()

    @pl.loop(1, COLS)
    def _(step):
        rows_copy(step).start()

    own = pltpu.make_async_copy(pair_ref.at[pl.ds(col * OWN, OWN)], rows.at[col], own_sem)
    own.start()
    proj_one_t = jnp.transpose(proj_one_ref[:, 2 * C :].astype(F32)).astype(BF16)
    proj_two_t = jnp.transpose(proj_two_ref[:, 2 * C :].astype(F32)).astype(BF16)
    bias_two_t = jnp.transpose(bias_two_ref[...].astype(F32)).astype(BF16)
    gain_two = gain_two_ref[...].astype(F32)
    head_of = lax.broadcasted_iota(jnp.int32, (LANES, C), 1) // DH
    for line in range(OWN):
        turned[line, C:, :] = jnp.ones((ONES, N), BF16)

    @pl.loop(1, 16)
    def _(step):
        plane_copy(step).wait_recv()

    for step in (1, 3, 2):
        ring_copy(step).start()
    pair_copy(0, x).start()

    own.wait()

    @pl.loop(1, COLS)
    def _(step):
        rows_copy(step).wait()

    def line_parts(line, values, gain, proj, proj_t):
        normed = layer_norm(values, gain).astype(BF16)
        parts = dot(normed, proj[:, : 2 * C])
        keys[line] = parts[:, C:].astype(BF16)
        for block in range(BLOCKS):
            here = slice(block * LANES, (block + 1) * LANES)
            values_f[line, block] = values[here]
            scaled = parts[here, :C] * (DH ** (-0.5) * LOG2E)
            for head in range(H):
                query[line, block, head * LANES : (head + 1) * LANES, :] = jnp.where(
                    head_of == head, scaled, 0.0
                ).astype(BF16)
        parts_t = dot_nt(proj_t, normed)
        turned[line, :C, :] = parts_t[:C].astype(BF16)
        gate = jax.nn.sigmoid(parts_t[C:])
        for block in range(BLOCKS):
            gate_f[line, block] = gate[:, block * LANES : (block + 1) * LANES]

    def attend(line, block, out):
        for head in range(H):
            here = slice(head * LANES, (head + 1) * LANES)
            score = dot_nt(keys[line], query[line, block, here, :]) + bias_f[head]
            top = jnp.max(score, axis=0, keepdims=True)
            prob[:, here] = jnp.exp2(score - top).astype(BF16)
        summed = dot(turned[line], prob[...])
        attn = jnp.concatenate(
            [
                summed[head * DH : (head + 1) * DH, head * LANES : (head + 1) * LANES]
                / summed[C : C + 1, head * LANES : (head + 1) * LANES]
                for head in range(H)
            ],
            axis=0,
        )
        gated = jnp.transpose(gate_f[line, block] * attn).astype(BF16)
        return values_f[line, block] + dot(gated, out)

    @pl.loop(0, OWN)
    def _(line):
        line_parts(line, rows[:, line].reshape(N, C).astype(F32), gain_one, proj_one_ref, proj_one_t)

    def plane_of(step):
        return lax.rem(x + jnp.where(step == 2, 3, jnp.where(step == 3, 2, step)), 4)

    def tile_copy(group):
        to = (lax.rem(group, ROWS), group // ROWS)
        return remote(tiles.at[group], columns.at[me], tile_send.at[group], tile_recv.at[me], to)

    def plane2_copy(block, step):
        mine = whole_two.at[x, ylo, z, yhi, core, pl.ds(block * 16, 16)]
        to = device_of(x, y + step // 4, z + lax.rem(step, 4), core)
        return remote(mine, mine, plane2_send.at[block, step], plane2_recv.at[block, step], to)

    def ring2_copy(block, step):
        slab = whole_two.at[x, :, :, :, core, pl.ds(block * 16, 16)]
        to = device_of(x + step, y, z, core)
        return remote(slab, slab, ring2_send.at[block, step], ring2_recv.at[block, step], to)

    def pair2_copy(block):
        slab = whole_two.at[:, :, :, :, core, pl.ds(block * 16, 16)]
        return remote(slab, slab, pair2_send.at[block], pair2_recv.at[block], sibling)

    def pass_on(block):
        @pl.loop(1, 16)
        def _(step):
            plane2_copy(block, step).wait_recv()

        for step in (1, 3, 2):
            ring2_copy(block, step).start()

    my_group = col * ROWS + row

    @pl.loop(0, BLOCKS)
    def _(step):
        block = plane_of(step)

        @pl.when(step == 1)
        def _():
            ring_copy(3).wait_recv()
            pair_copy(1, plane_of(1)).start()
            ring_copy(1).wait_recv()
            pair_copy(2, plane_of(2)).start()

        @pl.when(step == 2)
        def _():
            ring_copy(2).wait_recv()
            pair_copy(3, plane_of(3)).start()

        pair_copy(step, block).wait_recv()

        @pl.loop(0, COLS)
        def _(source):
            place = (source // 4, lax.rem(source // 2, 2), lax.rem(source, 2))
            one = whole_one[block, 0, *place].astype(F32) * LOG2E
            two = whole_one[block, 1, *place].astype(F32) * LOG2E
            lower = lax.broadcasted_iota(jnp.int32, (CHUNK, 128), 1) < 64
            left = jnp.where(lower, one, pltpu.roll(two, 64, 1))
            right = jnp.where(lower, pltpu.roll(one, 64, 1), two)
            for head in range(H):
                bias_f[head, pl.ds(source * 32, 16), :] = left[head * 16 : (head + 1) * 16]
                bias_f[head, pl.ds(source * 32 + 16, 16), :] = right[head * 16 : (head + 1) * 16]

        @pl.loop(0, OWN)
        def _(line):
            middle = attend(line, block, out_one_ref[...]).astype(BF16).astype(F32)
            line_f[...] = middle
            for place in range(OWN):
                flat_f[pl.ds(line * OWN + place, 32, 16), :] = line_f[pl.ds(place, 32, OWN), :]
            found = dot_nt(bias_two_t, layer_norm(middle, gain_two).astype(BF16))
            for head in range(H):
                small_f[pl.ds(head * OWN + line, 1), :] = found[head : head + 1]

        whole_two[x, ylo, z, yhi, core, pl.ds(block * 16, 16)] = small_f[...].astype(BF16)
        tiles[pl.ds(block * 32, 32)] = flat_f[:512].astype(BF16).reshape(32, 16, C)

        @pl.loop(1, 16)
        def _(step):
            plane2_copy(block, step).start()

        @pl.loop(0, 32)
        def _(group):
            @pl.when(block * 32 + group != my_group)
            def _():
                tile_copy(block * 32 + group).start()

        @pl.when(step >= 2)
        def _():
            pass_on(plane_of(step - 2))

    pass_on(plane_of(2))
    pass_on(plane_of(3))
    columns[me] = tiles[my_group]

    @pl.loop(0, DEVS)
    def _(source):
        @pl.when(source != me)
        def _():
            remote(
                tiles.at[0], columns.at[source], tile_send.at[0], tile_recv.at[source], sibling
            ).wait_recv()

    flat_f[...] = columns[...].reshape(DEVS * 16, C).astype(F32)

    @pl.loop(0, OWN)
    def _(line):
        line_parts(line, flat_f[pl.ds(line, N, OWN), :], gain_two, proj_two_ref, proj_two_t)

    for delta in (2, 1, 3, 0):
        block = lax.rem(x + delta, 4)
        for step in (1, 3, 2):
            ring2_copy(block, step).wait_recv()
        pair2_copy(block).start()

    def back_copy(other):
        return remote(
            result.at[other], landed.at[row], back_send.at[other], back_recv.at[row], (other, col)
        )

    @pl.loop(0, BLOCKS)
    def _(step):
        block = lax.rem(x + jnp.where(step == 0, 2, jnp.where(step == 2, 3, jnp.where(step == 3, 0, 1))), 4)
        pair2_copy(block).wait_recv()
        flat_f[...] = whole_two[:, :, :, :, :, pl.ds(block * 16, 16)].reshape(DEVS * 16, 128).astype(F32) * LOG2E
        for head in range(H):
            for line in range(OWN):
                bias_f[head, pl.ds(line, DEVS, OWN), :] = flat_f[pl.ds(head * OWN + line, DEVS, 16), :]

        @pl.loop(0, OWN)
        def _(line):
            flat_f[pl.ds(line, LANES, OWN), :] = attend(line, block, out_two_ref[...])

        result[pl.ds(block * 2, 2)] = flat_f[:512].astype(BF16).reshape(2, 256, C)
        for side in range(2):
            @pl.when(block * 2 + side != row)
            def _():
                back_copy(block * 2 + side).start()

    landed[row] = result[row]

    @pl.loop(0, ROWS)
    def _(source):
        @pl.when(source != row)
        def _():
            remote(
                result.at[0], landed.at[source], back_send.at[0], back_recv.at[source], sibling
            ).wait_recv()

    for source in range(ROWS):
        values_f[0, 0] = landed[source, :128].astype(F32)
        values_f[0, 1] = landed[source, 128:].astype(F32)
        for half in range(2):
            for place in range(OWN):
                flat_f[pl.ds(half * 1024 + source * OWN + place, 32, COLS_HERE), :] = values_f[
                    0, half, pl.ds(place, 32, OWN), :
                ]
    block_ref[...] = flat_f[...].astype(BF16).reshape(ROWS_HERE, COLS_HERE, C)

    @pl.loop(1, 16)
    def _(step):
        plane_copy(step).wait_send()

        @pl.loop(0, BLOCKS)
        def _(block):
            plane2_copy(block, step).wait_send()

    for step in range(1, 4):
        ring_copy(step).wait_send()
    for step in range(BLOCKS):
        pair_copy(step, plane_of(step)).wait_send()
        pair2_copy(step).wait_send()
        for delta in range(1, 4):
            ring2_copy(step, delta).wait_send()

    @pl.loop(0, DEVS)
    def _(group):
        @pl.when(group != my_group)
        def _():
            tile_copy(group).wait_send()

    @pl.loop(0, ROWS)
    def _(other):
        @pl.when(other != row)
        def _():
            back_copy(other).wait_send()


def body(pair, gain_one, proj_one, bias_one, out_one, gain_two, proj_two, bias_two, out_two):
    dma = pltpu.SemaphoreType.DMA
    gathered = pltpu.VMEM((4, 2, 4, 2, 2, CHUNK, 128), BF16)
    return pl.pallas_call(
        kernel,
        out_shape=jax.ShapeDtypeStruct((ROWS_HERE, COLS_HERE, C), BF16),
        in_specs=[VMEM] * 9,
        out_specs=VMEM,
        scratch_shapes=[
            pltpu.VMEM((COLS, OWN, COLS_HERE, C), BF16),
            gathered,
            gathered,
            pltpu.VMEM((DEVS, 16, C), BF16),
            pltpu.VMEM((DEVS, 16, C), BF16),
            pltpu.VMEM((ROWS, 256, C), BF16),
            pltpu.VMEM((ROWS, 256, C), BF16),
            pltpu.VMEM((DEVS * 16, C), F32),
            pltpu.VMEM((CHUNK, 128), F32),
            pltpu.VMEM((16, 128), F32),
            pltpu.VMEM((LANES, C), F32),
            pltpu.VMEM((H, N, LANES), F32),
            pltpu.VMEM((OWN, BLOCKS, LANES, C), F32),
            pltpu.VMEM((OWN, BLOCKS, H * LANES, C), BF16),
            pltpu.VMEM((OWN, N, C), BF16),
            pltpu.VMEM((OWN, C + ONES, N), BF16),
            pltpu.VMEM((OWN, BLOCKS, C, LANES), F32),
            pltpu.VMEM((N, H * LANES), BF16),
            dma, dma((COLS,)), dma((COLS,)),
            dma((16,)), dma((16,)), dma((4,)), dma((4,)), dma((4,)), dma((4,)),
            dma((DEVS,)), dma((DEVS,)),
            dma((BLOCKS, 16)), dma((BLOCKS, 16)), dma((BLOCKS, 4)), dma((BLOCKS, 4)),
            dma((BLOCKS,)), dma((BLOCKS,)),
            dma((ROWS,)), dma((ROWS,)),
        ],
        compiler_params=pltpu.CompilerParams(
            collective_id=0, has_side_effects=True, vmem_limit_bytes=48 * 1024 * 1024
        ),
        name="triangle",
    )(pair, gain_one.reshape(1, C), proj_one, bias_one, out_one, gain_two.reshape(1, C), proj_two, bias_two, out_two)


def solution(mesh):
    in_specs = (P("row", "col", None), P(), P(), P(), P(), P(), P(), P(), P())
    out_specs = P("row", "col", None)
    return jax.shard_map(body, mesh=mesh, in_specs=in_specs, out_specs=out_specs, check_vma=False)
```

time: 564 us -> 96.4 us (0.17)
  waiting for transfers between devices: 344 us -> 0 us
  Pallas kernels: 0 us -> 90.2 us
  matrix products: 53 us -> 0 us
  local copies, waits for them, and re-layouts: 56.1 us -> 5.13 us
  blocking collectives: 50.5 us -> 0 us
  other arithmetic: 42.1 us -> 0 us
  between operations: 13.7 us -> 0.03 us
    all_gather x6 -> x0, waiting for transfers between devices: 342 us -> none  [the longest x1 88.8 us: body(): lax.all_gather(keys, 'row', axis=0, tiled=True)]
    pallas_call x0 -> x1, Pallas kernels: none -> 90.2 us  [body(): pl.pallas_call(kernel, out_shape=jax.ShapeDtypeStruct((ROWS_HERE, COLS_HE...]
    dot_general x12 -> x0, matrix products: 53 us -> none  [the longest x1 11.7 us: body(): jnp.einsum('hijk,ikhd->ijhd', prob, value_heads, preferred_element_type=j...]
    all_gather x2 -> x0, blocking collectives: 50.5 us -> none  [full_bias(): banded = lax.all_gather(local_bias, 'col', axis=2, tiled=True)]
    all_gather x6 -> x0, local copies, waits for them, and re-layouts: 41.2 us -> none  [the longest x1 12 us: body(): lax.all_gather(values, 'col', axis=1, tiled=True)]
    sub x2 -> x0, other arithmetic: 36.3 us -> none  [body(): prob = jax.nn.softmax(score, axis=-1).astype(jnp.bfloat16)]
    reshape x3 -> x0, local copies, waits for them, and re-layouts: 8.66 us -> none  [the longest x2 4.64 us: body(): gated = (gate * attn.reshape(rows_here, cols_here, C)).astype(jnp.bfloat16)]
  transfers between devices with their start and end apart: 6 -> 0, of which waited for: 6 -> 0; matrix products, arithmetic and copies ran while one was open for 17% -> 0% of each run, Pallas kernels for 0% -> 0%
where the time goes in v1:
time: 96.4 us; the launch traced here: 95.4 us
  Pallas kernels  90.2 us (94%)
  local copies, waits for them, and re-layouts  5.13 us (5%)
    pallas_call x1, Pallas kernels, body(): pl.pallas_call(kernel, out_shape=jax.ShapeDtypeStruct((ROWS_HERE, COLS_HE...  90.2 us
    unnamed x21, local copies, waits for them, and re-layouts  5.13 us

profile of v1, /device:TPU:9, one launch (start us, length us, event | category | flops | bytes accessed | tf_op | source)
XLA Modules:
  0.0 95.4 jit_solution(12296221432851940597)
XLA Ops:
  0.0 0.0 copy-start.7
  0.0 0.0 copy-start.8
  0.0 0.7 copy-done.7
  0.7 0.0 copy-start.3
  0.7 0.0 copy-start.4
  0.7 0.1 copy.10.bias_one_ref
  0.8 0.0 copy-done.8
  0.8 0.0 copy-start.5
  0.8 0.0 copy-start.6
  0.8 0.1 copy.11.bias_two_ref
  1.0 0.5 copy-done.3
  1.4 0.0 copy-done.4
  1.5 0.0 copy-done.5
  1.5 0.0 copy-done.6
  1.5 0.0 copy-start
  1.5 1.0 %copy-done = bf16[64,32,128]{2,1,0:T(8,128)(2,1)S(1)} copy-done((bf16[64,32,128]{2,1,0:T(8,128)(2,1)S(1)}, bf16[64,32,128]{2,1,0:T(8,128)(2,1)}, u32[]{:S(2)}) %copy-start) | copy-done | bytes 524312
  2.5 0.0 copy-start.1
  2.5 0.9 copy-done.1
  3.5 0.0 copy-start.2
  3.5 0.9 copy-done.2
  4.4 90.2 %triangle.1 = bf16[64,32,128]{2,1,0:T(8,128)(2,1)S(1)} custom-call(bf16[64,32,128]{2,1,0:T(8,128)(2,1)S(1)} %copy-done, bf16[1,128]{1,0:T(2,128)(2,1)S(1)} %bitcast.2, bf16[128,512]{1,0:T(8,128)(2,1)S(1)} %copy-done.1, bf16[128,4]{1,0:T(8,128)(2,1)S(1)} %copy.10.bias_one_ref, bf16[128,128]{1,0:T(8,128)(2,1)S(1)} %copy-done.3, bf16[1,128]{1,0:T(2,128)(2,1)S(1)} %bitcast.3, ...), custom_call_target="tpu_custom_call" | custom-call | tf_op jit(solution)/shard_map/triangle/pallas_call | solution.py:379
  94.6 0.8 copy.13
Async XLA Ops:
  0.0 0.7 copy-start.7
  0.0 0.8 copy-start.8
  0.7 0.8 copy-start.3
  0.7 0.8 copy-start.4
  0.8 0.7 copy-start.5
  0.8 0.7 copy-start.6
  1.5 1.0 %copy-start = (bf16[64,32,128]{2,1,0:T(8,128)(2,1)S(1)}, bf16[64,32,128]{2,1,0:T(8,128)(2,1)}, u32[]{:S(2)}) copy-start(bf16[64,32,128]{2,1,0:T(8,128)(2,1)} %pair_ref.1) | copy-start | bytes 1572868
  2.5 0.9 copy-start.1
  3.5 0.9 copy-start.2

commit v2 on v1

--- a/solution.py
+++ b/solution.py
@@ -54,13 +54,15 @@
 
 
 def kernel(
+    pair_in, gain_one_in, proj_one_in, bias_one_in, out_one_in,
+    gain_two_in, proj_two_in, bias_two_in, out_two_in, landed,
     pair_ref, gain_one_ref, proj_one_ref, bias_one_ref, out_one_ref,
-    gain_two_ref, proj_two_ref, bias_two_ref, out_two_ref, block_ref,
-    rows, whole_one, whole_two, tiles, columns, result, landed,
+    gain_two_ref, proj_two_ref, bias_two_ref, out_two_ref, in_sem,
+    rows, whole_one, whole_two, tiles, columns, result,
     flat_f, chunk_f, small_f, line_f, bias_f, values_f, query, keys, turned, gate_f, prob,
     own_sem, rows_send, rows_recv, plane_send, plane_recv, ring_send, ring_recv, pair_send, pair_recv,
     tile_send, tile_recv, plane2_send, plane2_recv, ring2_send, ring2_recv, pair2_send, pair2_recv,
-    back_send, back_recv,
+    back_send, back_recv, joined,
 ):
     row, col = lax.axis_index("row"), lax.axis_index("col")
     me = row * COLS + col
@@ -71,15 +73,32 @@
 
     barrier = pltpu.get_barrier_semaphore()
 
-    @pl.loop(1, DEVS)
-    def _(step):
-        other = lax.rem(me + step, DEVS)
-        pl.semaphore_signal(
-            barrier, inc=1, device_id=(other // COLS, lax.rem(other, COLS)), device_id_type=MESH
-        )
+    @pl.loop(1, 32)
+    def _(step):
+        other = device_of(x, y + step // 8, z + lax.rem(step // 2, 4), core + lax.rem(step, 2))
+        pl.semaphore_signal(barrier, inc=1, device_id=other, device_id_type=MESH)
+
+    for step in range(1, 4):
+        pl.semaphore_signal(barrier, inc=1, device_id=device_of(x + step, y, z, core), device_id_type=MESH)
+
+    sources = (
+        pair_in, bias_one_in, gain_one_in, proj_one_in, out_one_in, gain_two_in, bias_two_in, proj_two_in, out_two_in
+    )
+    places = (
+        pair_ref, bias_one_ref, gain_one_ref, proj_one_ref, out_one_ref, gain_two_ref, bias_two_ref, proj_two_ref,
+        out_two_ref,
+    )
+    fetches = [
+        pltpu.make_async_copy(source, place, in_sem.at[index])
+        for index, (source, place) in enumerate(zip(sources, places))
+    ]
+    for fetch in fetches:
+        fetch.start()
+    for fetch in fetches[:3]:
+        fetch.wait()
 
     gain_one = gain_one_ref[...].astype(F32)
-    bias_one_t = jnp.transpose(bias_one_ref[...].astype(F32)).astype(BF16)
+    bias_one_t = bias_one_ref[...]
 
     @pl.loop(0, 8)
     def _(part):
@@ -95,7 +114,9 @@
             chunk_f[head * 16 + k, :] = found[head]
     whole_one[x, ylo, z, yhi, core] = chunk_f[...].astype(BF16)
 
-    pl.semaphore_wait(barrier, DEVS - 1)
+    pl.semaphore_wait(barrier, 34)
+    for step in range(1, 4):
+        pl.semaphore_signal(joined, inc=1, device_id=device_of(x + step, y, z, core), device_id_type=MESH)
 
     def plane_copy(step):
         mine = whole_one.at[x, ylo, z, yhi, core]
@@ -126,9 +147,11 @@
 
     own = pltpu.make_async_copy(pair_ref.at[pl.ds(col * OWN, OWN)], rows.at[col], own_sem)
     own.start()
+    for fetch in fetches[3:]:
+        fetch.wait()
     proj_one_t = jnp.transpose(proj_one_ref[:, 2 * C :].astype(F32)).astype(BF16)
     proj_two_t = jnp.transpose(proj_two_ref[:, 2 * C :].astype(F32)).astype(BF16)
-    bias_two_t = jnp.transpose(bias_two_ref[...].astype(F32)).astype(BF16)
+    bias_two_t = bias_two_ref[...]
     gain_two = gain_two_ref[...].astype(F32)
     head_of = lax.broadcasted_iota(jnp.int32, (LANES, C), 1) // DH
     for line in range(OWN):
@@ -166,23 +189,29 @@
         for block in range(BLOCKS):
             gate_f[line, block] = gate[:, block * LANES : (block + 1) * LANES]
 
-    def attend(line, block, out):
-        for head in range(H):
-            here = slice(head * LANES, (head + 1) * LANES)
-            score = dot_nt(keys[line], query[line, block, here, :]) + bias_f[head]
-            top = jnp.max(score, axis=0, keepdims=True)
-            prob[:, here] = jnp.exp2(score - top).astype(BF16)
-        summed = dot(turned[line], prob[...])
-        attn = jnp.concatenate(
-            [
-                summed[head * DH : (head + 1) * DH, head * LANES : (head + 1) * LANES]
-                / summed[C : C + 1, head * LANES : (head + 1) * LANES]
-                for head in range(H)
-            ],
-            axis=0,
-        )
-        gated = jnp.transpose(gate_f[line, block] * attn).astype(BF16)
-        return values_f[line, block] + dot(gated, out)
+    def attend(block, out):
+        for line in range(OWN):
+            for pair in range(H // 2):
+                both = dot_nt(keys[line], query[line, block, pair * 2 * LANES : (pair + 1) * 2 * LANES, :])
+                for side in range(2):
+                    head = pair * 2 + side
+                    score = both[:, side * LANES : (side + 1) * LANES] + bias_f[head]
+                    top = jnp.max(score, axis=0, keepdims=True)
+                    prob[line, :, head * LANES : (head + 1) * LANES] = jnp.exp2(score - top).astype(BF16)
+        gated = []
+        for line in range(OWN):
+            summed = dot(turned[line], prob[line])
+            attn = jnp.concatenate(
+                [
+                    summed[head * DH : (head + 1) * DH, head * LANES : (head + 1) * LANES]
+                    / summed[C : C + 1, head * LANES : (head + 1) * LANES]
+                    for head in range(H)
+                ],
+                axis=0,
+            )
+            gated.append(jnp.transpose(gate_f[line, block] * attn).astype(BF16))
+        update = dot(jnp.concatenate(gated, axis=0), out)
+        return jnp.concatenate([values_f[line, block] for line in range(OWN)], axis=0) + update
 
     @pl.loop(0, OWN)
     def _(line):
@@ -237,30 +266,34 @@
 
         pair_copy(step, block).wait_recv()
 
-        @pl.loop(0, COLS)
-        def _(source):
-            place = (source // 4, lax.rem(source // 2, 2), lax.rem(source, 2))
-            one = whole_one[block, 0, *place].astype(F32) * LOG2E
-            two = whole_one[block, 1, *place].astype(F32) * LOG2E
+        @pl.loop(0, 4)
+        def _(depth):
             lower = lax.broadcasted_iota(jnp.int32, (CHUNK, 128), 1) < 64
-            left = jnp.where(lower, one, pltpu.roll(two, 64, 1))
-            right = jnp.where(lower, pltpu.roll(one, 64, 1), two)
+            for part in range(4):
+                one = whole_one[block, 0, depth, part // 2, part % 2].astype(F32) * LOG2E
+                two = whole_one[block, 1, depth, part // 2, part % 2].astype(F32) * LOG2E
+                left = jnp.where(lower, one, pltpu.roll(two, 64, 1))
+                right = jnp.where(lower, pltpu.roll(one, 64, 1), two)
+                first = depth * 128 + part * 32
+                for head in range(H):
+                    bias_f[head, pl.ds(first, 16), :] = left[head * 16 : (head + 1) * 16]
+                    bias_f[head, pl.ds(first + 16, 16), :] = right[head * 16 : (head + 1) * 16]
+
+        middle = attend(block, out_one_ref[...]).astype(BF16).astype(F32)
+        line_f[...] = middle
+        for line in range(OWN):
+            for place in range(OWN):
+                flat_f[pl.ds(line * OWN + place, 32, 16), :] = line_f[pl.ds(line * LANES + place, 32, OWN), :]
+        found = dot_nt(bias_two_t, layer_norm(middle, gain_two).astype(BF16))
+        for line in range(OWN):
             for head in range(H):
-                bias_f[head, pl.ds(source * 32, 16), :] = left[head * 16 : (head + 1) * 16]
-                bias_f[head, pl.ds(source * 32 + 16, 16), :] = right[head * 16 : (head + 1) * 16]
-
-        @pl.loop(0, OWN)
-        def _(line):
-            middle = attend(line, block, out_one_ref[...]).astype(BF16).astype(F32)
-            line_f[...] = middle
-            for place in range(OWN):
-                flat_f[pl.ds(line * OWN + place, 32, 16), :] = line_f[pl.ds(place, 32, OWN), :]
-            found = dot_nt(bias_two_t, layer_norm(middle, gain_two).astype(BF16))
-            for head in range(H):
-                small_f[pl.ds(head * OWN + line, 1), :] = found[head : head + 1]
-
+                small_f[head * OWN + line, :] = found[head, line * LANES : (line + 1) * LANES]
         whole_two[x, ylo, z, yhi, core, pl.ds(block * 16, 16)] = small_f[...].astype(BF16)
         tiles[pl.ds(block * 32, 32)] = flat_f[:512].astype(BF16).reshape(32, 16, C)
+
+        @pl.when(step == 0)
+        def _():
+            pl.semaphore_wait(joined, 3)
 
         @pl.loop(1, 16)
         def _(step):
@@ -290,8 +323,7 @@
 
     flat_f[...] = columns[...].reshape(DEVS * 16, C).astype(F32)
 
-    @pl.loop(0, OWN)
-    def _(line):
+    for line in range(OWN):
         line_parts(line, flat_f[pl.ds(line, N, OWN), :], gain_two, proj_two_ref, proj_two_t)
 
     for delta in (2, 1, 3, 0):
@@ -314,17 +346,18 @@
             for line in range(OWN):
                 bias_f[head, pl.ds(line, DEVS, OWN), :] = flat_f[pl.ds(head * OWN + line, DEVS, 16), :]
 
-        @pl.loop(0, OWN)
-        def _(line):
-            flat_f[pl.ds(line, LANES, OWN), :] = attend(line, block, out_two_ref[...])
-
+        found = attend(block, out_two_ref[...])
+        for line in range(OWN):
+            flat_f[pl.ds(line, LANES, OWN), :] = found[line * LANES : (line + 1) * LANES]
         result[pl.ds(block * 2, 2)] = flat_f[:512].astype(BF16).reshape(2, 256, C)
         for side in range(2):
             @pl.when(block * 2 + side != row)
             def _():
                 back_copy(block * 2 + side).start()
 
-    landed[row] = result[row]
+    own_result = pltpu.make_async_copy(result.at[row], landed.at[row], own_sem)
+    own_result.start()
+    own_result.wait()
 
     @pl.loop(0, ROWS)
     def _(source):
@@ -333,16 +366,6 @@
             remote(
                 result.at[0], landed.at[source], back_send.at[0], back_recv.at[source], sibling
             ).wait_recv()
-
-    for source in range(ROWS):
-        values_f[0, 0] = landed[source, :128].astype(F32)
-        values_f[0, 1] = landed[source, 128:].astype(F32)
-        for half in range(2):
-            for place in range(OWN):
-                flat_f[pl.ds(half * 1024 + source * OWN + place, 32, COLS_HERE), :] = values_f[
-                    0, half, pl.ds(place, 32, OWN), :
-                ]
-    block_ref[...] = flat_f[...].astype(BF16).reshape(ROWS_HERE, COLS_HERE, C)
 
     @pl.loop(1, 16)
     def _(step):
@@ -373,45 +396,66 @@
             back_copy(other).wait_send()
 
 
+def arrange(landed_ref, block_ref, flat_f, block_f):
+    for source in range(ROWS):
+        flat_f[...] = landed_ref[source].astype(F32)
+        for place in range(OWN):
+            block_f[pl.ds(source * OWN + place, 16, COLS_HERE), :] = flat_f[pl.ds(place, 16, OWN), :]
+    block_ref[...] = block_f[...].astype(BF16).reshape(16, COLS_HERE, C)
+
+
 def body(pair, gain_one, proj_one, bias_one, out_one, gain_two, proj_two, bias_two, out_two):
     dma = pltpu.SemaphoreType.DMA
     gathered = pltpu.VMEM((4, 2, 4, 2, 2, CHUNK, 128), BF16)
-    return pl.pallas_call(
+    landed = pl.pallas_call(
         kernel,
-        out_shape=jax.ShapeDtypeStruct((ROWS_HERE, COLS_HERE, C), BF16),
-        in_specs=[VMEM] * 9,
-        out_specs=VMEM,
+        out_shape=jax.ShapeDtypeStruct((ROWS, 256, C), BF16),
+        in_specs=[pl.BlockSpec(memory_space=pltpu.HBM)] * 9,
+        out_specs=pl.BlockSpec(memory_space=pl.ANY),
         scratch_shapes=[
+            pltpu.VMEM((ROWS_HERE, COLS_HERE, C), BF16),
+            pltpu.VMEM((1, C), BF16),
+            pltpu.VMEM((C, 4 * C), BF16),
+            pltpu.VMEM((H, C), BF16),
+            pltpu.VMEM((C, C), BF16),
+            pltpu.VMEM((1, C), BF16),
+            pltpu.VMEM((C, 4 * C), BF16),
+            pltpu.VMEM((H, C), BF16),
+            pltpu.VMEM((C, C), BF16),
+            dma((9,)),
             pltpu.VMEM((COLS, OWN, COLS_HERE, C), BF16),
             gathered,
             gathered,
             pltpu.VMEM((DEVS, 16, C), BF16),
             pltpu.VMEM((DEVS, 16, C), BF16),
             pltpu.VMEM((ROWS, 256, C), BF16),
-            pltpu.VMEM((ROWS, 256, C), BF16),
             pltpu.VMEM((DEVS * 16, C), F32),
             pltpu.VMEM((CHUNK, 128), F32),
             pltpu.VMEM((16, 128), F32),
-            pltpu.VMEM((LANES, C), F32),
+            pltpu.VMEM((OWN * LANES, C), F32),
             pltpu.VMEM((H, N, LANES), F32),
             pltpu.VMEM((OWN, BLOCKS, LANES, C), F32),
             pltpu.VMEM((OWN, BLOCKS, H * LANES, C), BF16),
             pltpu.VMEM((OWN, N, C), BF16),
             pltpu.VMEM((OWN, C + ONES, N), BF16),
             pltpu.VMEM((OWN, BLOCKS, C, LANES), F32),
-            pltpu.VMEM((N, H * LANES), BF16),
+            pltpu.VMEM((OWN, N, H * LANES), BF16),
             dma, dma((COLS,)), dma((COLS,)),
             dma((16,)), dma((16,)), dma((4,)), dma((4,)), dma((4,)), dma((4,)),
             dma((DEVS,)), dma((DEVS,)),
             dma((BLOCKS, 16)), dma((BLOCKS, 16)), dma((BLOCKS, 4)), dma((BLOCKS, 4)),
             dma((BLOCKS,)), dma((BLOCKS,)),
-            dma((ROWS,)), dma((ROWS,)),
+            dma((ROWS,)), dma((ROWS,)), pltpu.SemaphoreType.REGULAR,
         ],
         compiler_params=pltpu.CompilerParams(
-            collective_id=0, has_side_effects=True, vmem_limit_bytes=48 * 1024 * 1024
+            collective_id=0, has_side_effects=True, vmem_limit_bytes=60 * 1024 * 1024
         ),
         name="triangle",
-    )(pair, gain_one.reshape(1, C), proj_one, bias_one, out_one, gain_two.reshape(1, C), proj_two, bias_two, out_two)
+    )(
+        pair, gain_one.reshape(1, C), proj_one, bias_one.T, out_one,
+        gain_two.reshape(1, C), proj_two, bias_two.T, out_two,
+    )
+    return landed.reshape(ROWS, ROWS_HERE, OWN, C).transpose(1, 0, 2, 3).reshape(ROWS_HERE, COLS_HERE, C)
 
 
 def solution(mesh):

time: 96.4 us -> 69.5 us (0.72)
  Pallas kernels: 90.2 us -> 67.3 us
  local copies, waits for them, and re-layouts: 5.13 us -> 2.02 us
    pallas_call x1, Pallas kernels: 90.2 us -> 67.3 us  [body(): pl.pallas_call(kernel, out_shape=jax.ShapeDtypeStruct((ROWS, 256, C), BF1...]
    unnamed x21 -> x0, local copies, waits for them, and re-layouts: 5.13 us -> none
    transpose x0 -> x1, local copies, waits for them, and re-layouts: none -> 2.02 us  [body(): landed.reshape(ROWS, ROWS_HERE, OWN, C).transpose(1, 0, 2, 3)]
where the time goes in v2:
time: 69.5 us; the launch traced here: 69.3 us
  Pallas kernels  67.3 us (97%)
  local copies, waits for them, and re-layouts  2.02 us (3%)
    pallas_call x1, Pallas kernels, body(): pl.pallas_call(kernel, out_shape=jax.ShapeDtypeStruct((ROWS, 256, C), BF1...  67.3 us
    transpose x1, local copies, waits for them, and re-layouts, body(): landed.reshape(ROWS, ROWS_HERE, OWN, C).transpose(1, 0, 2, 3)  2.02 us

profile of v2, /device:TPU:9, one launch (start us, length us, event | category | flops | bytes accessed | tf_op | source)
XLA Modules:
  0.0 69.3 jit_solution(357697849552450764)
XLA Ops:
  0.0 67.3 %triangle.1 = bf16[8,256,128]{2,1,0:T(8,128)(2,1)} custom-call(bf16[64,32,128]{2,1,0:T(8,128)(2,1)} %pair_in.1, bf16[1,128]{1,0:T(2,128)(2,1)} %bitcast.11, bf16[128,512]{1,0:T(8,128)(2,1)} %proj_one_in.1, bf16[4,128]{1,0:T(4,128)(2,1)} %bitcast.9, bf16[128,128]{1,0:T(8,128)(2,1)} %out_one_in.1, bf16[1,128]{1,0:T(2,128)(2,1)} %bitcast.12, ...), custom_call_target="tpu_custom_call" | custom-call | tf_op jit(solution)/shard_map/triangle/pallas_call | solution.py:410
  67.3 2.0 %copy.10 = bf16[64,8,4,128]{3,2,1,0:T(4,128)(2,1)} copy(bf16[64,8,4,128]{3,2,0,1:T(4,128)(2,1)} %bitcast.8) | data formatting | bytes 1048576 | tf_op jit(solution)/shard_map/transpose | solution.py:458

commit v3 on v2

--- a/solution.py
+++ b/solution.py
@@ -118,15 +118,19 @@
     for step in range(1, 4):
         pl.semaphore_signal(joined, inc=1, device_id=device_of(x + step, y, z, core), device_id_type=MESH)
 
+    def many(count, send_sem, recv_sem):
+        some = pl.ds(0, count)
+        return remote(tiles.at[some], columns.at[some], send_sem, recv_sem, sibling)
+
     def plane_copy(step):
         mine = whole_one.at[x, ylo, z, yhi, core]
         to = device_of(x, y + step // 4, z + lax.rem(step, 4), core)
-        return remote(mine, mine, plane_send.at[step], plane_recv.at[step], to)
+        return remote(mine, mine, plane_send, plane_recv, to)
 
     def rows_copy(step):
         other = lax.rem(col + step, COLS)
         return remote(
-            pair_ref.at[pl.ds(other * OWN, OWN)], rows.at[col], rows_send.at[step], rows_recv.at[step], (row, other)
+            pair_ref.at[pl.ds(other * OWN, OWN)], rows.at[col], rows_send, rows_recv, (row, other)
         )
 
     def ring_copy(step):
@@ -157,9 +161,7 @@
     for line in range(OWN):
         turned[line, C:, :] = jnp.ones((ONES, N), BF16)
 
-    @pl.loop(1, 16)
-    def _(step):
-        plane_copy(step).wait_recv()
+    many(60, plane_send, plane_recv).wait_recv()
 
     for step in (1, 3, 2):
         ring_copy(step).start()
@@ -167,9 +169,7 @@
 
     own.wait()
 
-    @pl.loop(1, COLS)
-    def _(step):
-        rows_copy(step).wait()
+    many(120, rows_send, rows_recv).wait()
 
     def line_parts(line, values, gain, proj, proj_t):
         normed = layer_norm(values, gain).astype(BF16)
@@ -213,8 +213,7 @@
         update = dot(jnp.concatenate(gated, axis=0), out)
         return jnp.concatenate([values_f[line, block] for line in range(OWN)], axis=0) + update
 
-    @pl.loop(0, OWN)
-    def _(line):
+    for line in range(OWN):
         line_parts(line, rows[:, line].reshape(N, C).astype(F32), gain_one, proj_one_ref, proj_one_t)
 
     def plane_of(step):
@@ -222,27 +221,27 @@
 
     def tile_copy(group):
         to = (lax.rem(group, ROWS), group // ROWS)
-        return remote(tiles.at[group], columns.at[me], tile_send.at[group], tile_recv.at[me], to)
+        return remote(tiles.at[group], columns.at[me], tile_send, tile_recv, to)
+
+    def all_tiles():
+        return many(DEVS - 1, tile_send, tile_recv)
 
     def plane2_copy(block, step):
         mine = whole_two.at[x, ylo, z, yhi, core, pl.ds(block * 16, 16)]
         to = device_of(x, y + step // 4, z + lax.rem(step, 4), core)
-        return remote(mine, mine, plane2_send.at[block, step], plane2_recv.at[block, step], to)
+        return remote(mine, mine, plane2_send.at[block], plane2_recv.at[block], to)
 
     def ring2_copy(block, step):
         slab = whole_two.at[x, :, :, :, core, pl.ds(block * 16, 16)]
         to = device_of(x + step, y, z, core)
-        return remote(slab, slab, ring2_send.at[block, step], ring2_recv.at[block, step], to)
+        return remote(slab, slab, ring2_send.at[block], ring2_recv.at[block], to)
 
     def pair2_copy(block):
         slab = whole_two.at[:, :, :, :, core, pl.ds(block * 16, 16)]
         return remote(slab, slab, pair2_send.at[block], pair2_recv.at[block], sibling)
 
     def pass_on(block):
-        @pl.loop(1, 16)
-        def _(step):
-            plane2_copy(block, step).wait_recv()
-
+        many(15, plane2_send.at[block], plane2_recv.at[block]).wait_recv()
         for step in (1, 3, 2):
             ring2_copy(block, step).start()
 
@@ -280,16 +279,11 @@
                     bias_f[head, pl.ds(first + 16, 16), :] = right[head * 16 : (head + 1) * 16]
 
         middle = attend(block, out_one_ref[...]).astype(BF16).astype(F32)
-        line_f[...] = middle
-        for line in range(OWN):
-            for place in range(OWN):
-                flat_f[pl.ds(line * OWN + place, 32, 16), :] = line_f[pl.ds(line * LANES + place, 32, OWN), :]
         found = dot_nt(bias_two_t, layer_norm(middle, gain_two).astype(BF16))
         for line in range(OWN):
             for head in range(H):
                 small_f[head * OWN + line, :] = found[head, line * LANES : (line + 1) * LANES]
         whole_two[x, ylo, z, yhi, core, pl.ds(block * 16, 16)] = small_f[...].astype(BF16)
-        tiles[pl.ds(block * 32, 32)] = flat_f[:512].astype(BF16).reshape(32, 16, C)
 
         @pl.when(step == 0)
         def _():
@@ -298,6 +292,12 @@
         @pl.loop(1, 16)
         def _(step):
             plane2_copy(block, step).start()
+
+        line_f[...] = middle
+        for line in range(OWN):
+            for place in range(OWN):
+                flat_f[pl.ds(line * OWN + place, 32, 16), :] = line_f[pl.ds(line * LANES + place, 32, OWN), :]
+        tiles[pl.ds(block * 32, 32)] = flat_f[:512].astype(BF16).reshape(32, 16, C)
 
         @pl.loop(0, 32)
         def _(group):
@@ -313,28 +313,24 @@
     pass_on(plane_of(3))
     columns[me] = tiles[my_group]
 
-    @pl.loop(0, DEVS)
-    def _(source):
-        @pl.when(source != me)
-        def _():
-            remote(
-                tiles.at[0], columns.at[source], tile_send.at[0], tile_recv.at[source], sibling
-            ).wait_recv()
-
+    all_tiles().wait_recv()
     flat_f[...] = columns[...].reshape(DEVS * 16, C).astype(F32)
+
+    def to_other_core(delta):
+        block = lax.rem(x + delta, 4)
+        many(48, ring2_send.at[block], ring2_recv.at[block]).wait_recv()
+        pair2_copy(block).start()
 
     for line in range(OWN):
         line_parts(line, flat_f[pl.ds(line, N, OWN), :], gain_two, proj_two_ref, proj_two_t)
-
-    for delta in (2, 1, 3, 0):
-        block = lax.rem(x + delta, 4)
-        for step in (1, 3, 2):
-            ring2_copy(block, step).wait_recv()
-        pair2_copy(block).start()
+        if line == 1:
+            to_other_core(2)
+    for delta in (1, 3, 0):
+        to_other_core(delta)
 
     def back_copy(other):
         return remote(
-            result.at[other], landed.at[row], back_send.at[other], back_recv.at[row], (other, col)
+            result.at[other], landed.at[row], back_send, back_recv, (other, col)
         )
 
     @pl.loop(0, BLOCKS)
@@ -359,41 +355,19 @@
     own_result.start()
     own_result.wait()
 
-    @pl.loop(0, ROWS)
-    def _(source):
-        @pl.when(source != row)
-        def _():
-            remote(
-                result.at[0], landed.at[source], back_send.at[0], back_recv.at[source], sibling
-            ).wait_recv()
-
-    @pl.loop(1, 16)
-    def _(step):
-        plane_copy(step).wait_send()
-
-        @pl.loop(0, BLOCKS)
-        def _(block):
-            plane2_copy(block, step).wait_send()
-
+    many(60, plane_send, plane_recv).wait_send()
     for step in range(1, 4):
         ring_copy(step).wait_send()
     for step in range(BLOCKS):
         pair_copy(step, plane_of(step)).wait_send()
-        pair2_copy(step).wait_send()
-        for delta in range(1, 4):
-            ring2_copy(step, delta).wait_send()
-
-    @pl.loop(0, DEVS)
-    def _(group):
-        @pl.when(group != my_group)
-        def _():
-            tile_copy(group).wait_send()
-
-    @pl.loop(0, ROWS)
-    def _(other):
-        @pl.when(other != row)
-        def _():
-            back_copy(other).wait_send()
+        many(64, pair2_send.at[step], pair2_recv.at[step]).wait_send()
+        many(15, plane2_send.at[step], plane2_recv.at[step]).wait_send()
+        many(48, ring2_send.at[step], ring2_recv.at[step]).wait_send()
+    all_tiles().wait_send()
+
+    all_back = many(7 * 16, back_send, back_recv)
+    all_back.wait_recv()
+    all_back.wait_send()
 
 
 def arrange(landed_ref, block_ref, flat_f, block_f):
@@ -440,12 +414,11 @@
             pltpu.VMEM((OWN, C + ONES, N), BF16),
             pltpu.VMEM((OWN, BLOCKS, C, LANES), F32),
             pltpu.VMEM((OWN, N, H * LANES), BF16),
-            dma, dma((COLS,)), dma((COLS,)),
-            dma((16,)), dma((16,)), dma((4,)), dma((4,)), dma((4,)), dma((4,)),
-            dma((DEVS,)), dma((DEVS,)),
-            dma((BLOCKS, 16)), dma((BLOCKS, 16)), dma((BLOCKS, 4)), dma((BLOCKS, 4)),
-            dma((BLOCKS,)), dma((BLOCKS,)),
-            dma((ROWS,)), dma((ROWS,)), pltpu.SemaphoreType.REGULAR,
+            dma, dma, dma,
+            dma, dma, dma((4,)), dma((4,)), dma((4,)), dma((4,)),
+            dma, dma,
+            dma((BLOCKS,)), dma((BLOCKS,)), dma((BLOCKS,)), dma((BLOCKS,)), dma((BLOCKS,)), dma((BLOCKS,)),
+            dma, dma, pltpu.SemaphoreType.REGULAR,
         ],
         compiler_params=pltpu.CompilerParams(
             collective_id=0, has_side_effects=True, vmem_limit_bytes=60 * 1024 * 1024

time: 69.5 us -> 63.5 us (0.914)
  Pallas kernels: 67.3 us -> 61.3 us
    pallas_call x1, Pallas kernels: 67.3 us -> 61.3 us  [body(): pl.pallas_call(kernel, out_shape=jax.ShapeDtypeStruct((ROWS, 256, C), BF1...]
where the time goes in v3:
time: 63.5 us; the launch traced here: 63.3 us
  Pallas kernels  61.3 us (97%)
  local copies, waits for them, and re-layouts  2.02 us (3%)
    pallas_call x1, Pallas kernels, body(): pl.pallas_call(kernel, out_shape=jax.ShapeDtypeStruct((ROWS, 256, C), BF1...  61.3 us
    transpose x1, local copies, waits for them, and re-layouts, body(): landed.reshape(ROWS, ROWS_HERE, OWN, C).transpose(1, 0, 2, 3)  2.02 us

profile of v3, /device:TPU:9, one launch (start us, length us, event | category | flops | bytes accessed | tf_op | source)
XLA Modules:
  0.0 63.3 jit_solution(15913031024674868655)
XLA Ops:
  0.0 61.3 %triangle.1 = bf16[8,256,128]{2,1,0:T(8,128)(2,1)} custom-call(bf16[64,32,128]{2,1,0:T(8,128)(2,1)} %pair_in.1, bf16[1,128]{1,0:T(2,128)(2,1)} %bitcast.11, bf16[128,512]{1,0:T(8,128)(2,1)} %proj_one_in.1, bf16[4,128]{1,0:T(4,128)(2,1)} %bitcast.9, bf16[128,128]{1,0:T(8,128)(2,1)} %out_one_in.1, bf16[1,128]{1,0:T(2,128)(2,1)} %bitcast.12, ...), custom_call_target="tpu_custom_call" | custom-call | tf_op jit(solution)/shard_map/triangle/pallas_call | solution.py:384
  61.3 2.0 %copy.10 = bf16[64,8,4,128]{3,2,1,0:T(4,128)(2,1)} copy(bf16[64,8,4,128]{3,2,0,1:T(4,128)(2,1)} %bitcast.8) | data formatting | bytes 1048576 | tf_op jit(solution)/shard_map/transpose | solution.py:431

commit v4 on v3

--- a/solution.py
+++ b/solution.py
@@ -21,6 +21,7 @@
 ONES = 16
 LOG2E = 1.4426950408889634
 MESH = pl.DeviceIdType.MESH
+FAR_FIRST = sorted(range(1, 16), key=lambda step: -min(step // 4, 4 - step // 4) - min(step % 4, 4 - step % 4))
 F32 = jnp.float32
 BF16 = jnp.bfloat16
 VMEM = pl.BlockSpec(memory_space=pltpu.VMEM)
@@ -72,15 +73,6 @@
     sibling = (row, col + 1 - 2 * core)
 
     barrier = pltpu.get_barrier_semaphore()
-
-    @pl.loop(1, 32)
-    def _(step):
-        other = device_of(x, y + step // 8, z + lax.rem(step // 2, 4), core + lax.rem(step, 2))
-        pl.semaphore_signal(barrier, inc=1, device_id=other, device_id_type=MESH)
-
-    for step in range(1, 4):
-        pl.semaphore_signal(barrier, inc=1, device_id=device_of(x + step, y, z, core), device_id_type=MESH)
-
     sources = (
         pair_in, bias_one_in, gain_one_in, proj_one_in, out_one_in, gain_two_in, bias_two_in, proj_two_in, out_two_in
     )
@@ -94,6 +86,15 @@
     ]
     for fetch in fetches:
         fetch.start()
+
+    @pl.loop(1, 32)
+    def _(step):
+        other = device_of(x, y + step // 8, z + lax.rem(step // 2, 4), core + lax.rem(step, 2))
+        pl.semaphore_signal(barrier, inc=1, device_id=other, device_id_type=MESH)
+
+    for step in range(1, 4):
+        pl.semaphore_signal(barrier, inc=1, device_id=device_of(x + step, y, z, core), device_id_type=MESH)
+
     for fetch in fetches[:3]:
         fetch.wait()
 
@@ -137,16 +138,20 @@
         slab = whole_one.at[x, :, :, :, core]
         return remote(slab, slab, ring_send.at[step], ring_recv.at[step], device_of(x + step, y, z, core))
 
+    def onward_copy(step):
+        half = pl.ds(0, CHUNK // 2) if step == 1 else pl.ds(CHUNK // 2, CHUNK // 2)
+        slab = whole_one.at[lax.rem(x + 4 - step, 4), :, :, :, core, half]
+        to = device_of(x + step, y, z, core)
+        return remote(slab, slab, ring_send.at[step - 1], ring_recv.at[step - 1], to)
+
     def pair_copy(step, plane):
         slab = whole_one.at[plane, :, :, :, core]
         return remote(slab, slab, pair_send.at[step], pair_recv.at[step], sibling)
 
-    @pl.loop(1, 16)
-    def _(step):
+    for step in FAR_FIRST:
         plane_copy(step).start()
 
-    @pl.loop(1, COLS)
-    def _(step):
+    for step in sorted(range(1, COLS), key=lambda step: -min(step // 4, 4 - step // 4)):
         rows_copy(step).start()
 
     own = pltpu.make_async_copy(pair_ref.at[pl.ds(col * OWN, OWN)], rows.at[col], own_sem)
@@ -163,7 +168,7 @@
 
     many(60, plane_send, plane_recv).wait_recv()
 
-    for step in (1, 3, 2):
+    for step in (1, 3):
         ring_copy(step).start()
     pair_copy(0, x).start()
 
@@ -189,7 +194,7 @@
         for block in range(BLOCKS):
             gate_f[line, block] = gate[:, block * LANES : (block + 1) * LANES]
 
-    def attend(block, out):
+    def attend(block, out, between):
         for line in range(OWN):
             for pair in range(H // 2):
                 both = dot_nt(keys[line], query[line, block, pair * 2 * LANES : (pair + 1) * 2 * LANES, :])
@@ -198,17 +203,15 @@
                     score = both[:, side * LANES : (side + 1) * LANES] + bias_f[head]
                     top = jnp.max(score, axis=0, keepdims=True)
                     prob[line, :, head * LANES : (head + 1) * LANES] = jnp.exp2(score - top).astype(BF16)
+        between()
         gated = []
         for line in range(OWN):
-            summed = dot(turned[line], prob[line])
-            attn = jnp.concatenate(
-                [
-                    summed[head * DH : (head + 1) * DH, head * LANES : (head + 1) * LANES]
-                    / summed[C : C + 1, head * LANES : (head + 1) * LANES]
-                    for head in range(H)
-                ],
-                axis=0,
-            )
+            attn = []
+            for head in range(H):
+                lhs = jnp.concatenate([turned[line, head * DH : (head + 1) * DH, :], turned[line, C:, :]], axis=0)
+                summed = dot(lhs, prob[line, :, head * LANES : (head + 1) * LANES])
+                attn.append(summed[:DH] * (1.0 / summed[DH : DH + 1]))
+            attn = jnp.concatenate(attn, axis=0)
             gated.append(jnp.transpose(gate_f[line, block] * attn).astype(BF16))
         update = dot(jnp.concatenate(gated, axis=0), out)
         return jnp.concatenate([values_f[line, block] for line in range(OWN)], axis=0) + update
@@ -226,42 +229,40 @@
     def all_tiles():
         return many(DEVS - 1, tile_send, tile_recv)
 
-    def plane2_copy(block, step):
-        mine = whole_two.at[x, ylo, z, yhi, core, pl.ds(block * 16, 16)]
-        to = device_of(x, y + step // 4, z + lax.rem(step, 4), core)
-        return remote(mine, mine, plane2_send.at[block], plane2_recv.at[block], to)
-
-    def ring2_copy(block, step):
-        slab = whole_two.at[x, :, :, :, core, pl.ds(block * 16, 16)]
-        to = device_of(x + step, y, z, core)
-        return remote(slab, slab, ring2_send.at[block], ring2_recv.at[block], to)
-
-    def pair2_copy(block):
-        slab = whole_two.at[:, :, :, :, core, pl.ds(block * 16, 16)]
-        return remote(slab, slab, pair2_send.at[block], pair2_recv.at[block], sibling)
-
-    def pass_on(block):
-        many(15, plane2_send.at[block], plane2_recv.at[block]).wait_recv()
-        for step in (1, 3, 2):
-            ring2_copy(block, step).start()
+    def at_step(step):
+        return pl.ds(step * 16, 16)
+
+    def plane2_copy(axis, step, index):
+        mine = whole_two.at[x, ylo, z, yhi, core, at_step(step)]
+        one, two = index // 4, index % 4
+        to = device_of(x + one, y, z + two, core) if axis == "y" else device_of(x + one, y + two, z, core)
+        return remote(mine, mine, plane2_send.at[step], plane2_recv.at[step], to)
+
+    def ring2_copy(axis, step, index):
+        if axis == "y":
+            slab, to = whole_two.at[:, ylo, :, yhi, core, at_step(step)], device_of(x, y + index, z, core)
+        else:
+            slab, to = whole_two.at[:, :, z, :, core, at_step(step)], device_of(x, y, z + index, core)
+        return remote(slab, slab, ring2_send.at[step], ring2_recv.at[step], to)
+
+    def pair2_copy(step):
+        slab = whole_two.at[:, :, :, :, core, at_step(step)]
+        return remote(slab, slab, pair2_send.at[step], pair2_recv.at[step], sibling)
+
+    def pass_on(axis, step):
+        many(15, plane2_send.at[step], plane2_recv.at[step]).wait_recv()
+        for index in (1, 3, 2):
+            ring2_copy(axis, step, index).start()
+
+    def to_other_core(step):
+        many(48, ring2_send.at[step], ring2_recv.at[step]).wait_recv()
+        pair2_copy(step).start()
 
     my_group = col * ROWS + row
 
     @pl.loop(0, BLOCKS)
     def _(step):
         block = plane_of(step)
-
-        @pl.when(step == 1)
-        def _():
-            ring_copy(3).wait_recv()
-            pair_copy(1, plane_of(1)).start()
-            ring_copy(1).wait_recv()
-            pair_copy(2, plane_of(2)).start()
-
-        @pl.when(step == 2)
-        def _():
-            ring_copy(2).wait_recv()
-            pair_copy(3, plane_of(3)).start()
 
         pair_copy(step, block).wait_recv()
 
@@ -278,20 +279,38 @@
                     bias_f[head, pl.ds(first, 16), :] = left[head * 16 : (head + 1) * 16]
                     bias_f[head, pl.ds(first + 16, 16), :] = right[head * 16 : (head + 1) * 16]
 
-        middle = attend(block, out_one_ref[...]).astype(BF16).astype(F32)
+        def fetch_next():
+            @pl.when(step == 0)
+            def _():
+                ring_copy(3).wait_recv()
+                onward_copy(3).start()
+                pair_copy(1, plane_of(1)).start()
+                ring_copy(1).wait_recv()
+                onward_copy(1).start()
+                pair_copy(2, plane_of(2)).start()
+
+            @pl.when(step == 1)
+            def _():
+                onward_copy(1).wait_recv()
+                onward_copy(3).wait_recv()
+                pair_copy(3, plane_of(3)).start()
+
+        middle = attend(block, out_one_ref[...], fetch_next).astype(BF16).astype(F32)
         found = dot_nt(bias_two_t, layer_norm(middle, gain_two).astype(BF16))
         for line in range(OWN):
             for head in range(H):
                 small_f[head * OWN + line, :] = found[head, line * LANES : (line + 1) * LANES]
-        whole_two[x, ylo, z, yhi, core, pl.ds(block * 16, 16)] = small_f[...].astype(BF16)
+        whole_two[x, ylo, z, yhi, core, at_step(step)] = small_f[...].astype(BF16)
 
         @pl.when(step == 0)
         def _():
             pl.semaphore_wait(joined, 3)
 
-        @pl.loop(1, 16)
-        def _(step):
-            plane2_copy(block, step).start()
+        for parity, axis in enumerate("yz"):
+            @pl.when(lax.rem(step, 2) == parity)
+            def _():
+                for index in FAR_FIRST:
+                    plane2_copy(axis, step, index).start()
 
         line_f[...] = middle
         for line in range(OWN):
@@ -299,34 +318,34 @@
                 flat_f[pl.ds(line * OWN + place, 32, 16), :] = line_f[pl.ds(line * LANES + place, 32, OWN), :]
         tiles[pl.ds(block * 32, 32)] = flat_f[:512].astype(BF16).reshape(32, 16, C)
 
-        @pl.loop(0, 32)
-        def _(group):
-            @pl.when(block * 32 + group != my_group)
-            def _():
-                tile_copy(block * 32 + group).start()
-
-        @pl.when(step >= 2)
-        def _():
-            pass_on(plane_of(step - 2))
-
-    pass_on(plane_of(2))
-    pass_on(plane_of(3))
+        @pl.loop(0, 32, unroll=8)
+        def _(index):
+            group = block * 32 + lax.rem(index + me, 32)
+
+            @pl.when(group != my_group)
+            def _():
+                tile_copy(group).start()
+
+        for late, axis in ((2, "y"), (3, "z")):
+            @pl.when(step == late)
+            def _():
+                pass_on(axis, late - 2)
+
+    pass_on("y", 2)
+    to_other_core(0)
+    pass_on("z", 3)
+    to_other_core(1)
     columns[me] = tiles[my_group]
 
     all_tiles().wait_recv()
     flat_f[...] = columns[...].reshape(DEVS * 16, C).astype(F32)
 
-    def to_other_core(delta):
-        block = lax.rem(x + delta, 4)
-        many(48, ring2_send.at[block], ring2_recv.at[block]).wait_recv()
-        pair2_copy(block).start()
-
     for line in range(OWN):
         line_parts(line, flat_f[pl.ds(line, N, OWN), :], gain_two, proj_two_ref, proj_two_t)
-        if line == 1:
-            to_other_core(2)
-    for delta in (1, 3, 0):
-        to_other_core(delta)
+    for step in (2, 3):
+        to_other_core(step)
+    for step in range(BLOCKS):
+        pair2_copy(step).wait_recv()
 
     def back_copy(other):
         return remote(
@@ -336,13 +355,17 @@
     @pl.loop(0, BLOCKS)
     def _(step):
         block = lax.rem(x + jnp.where(step == 0, 2, jnp.where(step == 2, 3, jnp.where(step == 3, 0, 1))), 4)
-        pair2_copy(block).wait_recv()
-        flat_f[...] = whole_two[:, :, :, :, :, pl.ds(block * 16, 16)].reshape(DEVS * 16, 128).astype(F32) * LOG2E
+        for plane in range(4):
+            delta = lax.rem(block - plane + 4, 4)
+            made = jnp.where(delta == 2, 3, jnp.where(delta == 3, 2, delta))
+            flat_f[plane * 512 : (plane + 1) * 512, :] = (
+                whole_two[plane, :, :, :, :, at_step(made)].reshape(512, 128).astype(F32) * LOG2E
+            )
         for head in range(H):
             for line in range(OWN):
                 bias_f[head, pl.ds(line, DEVS, OWN), :] = flat_f[pl.ds(head * OWN + line, DEVS, 16), :]
 
-        found = attend(block, out_two_ref[...])
+        found = attend(block, out_two_ref[...], lambda: None)
         for line in range(OWN):
             flat_f[pl.ds(line, LANES, OWN), :] = found[line * LANES : (line + 1) * LANES]
         result[pl.ds(block * 2, 2)] = flat_f[:512].astype(BF16).reshape(2, 256, C)
@@ -356,8 +379,9 @@
     own_result.wait()
 
     many(60, plane_send, plane_recv).wait_send()
-    for step in range(1, 4):
+    for step in (1, 3):
         ring_copy(step).wait_send()
+        onward_copy(step).wait_send()
     for step in range(BLOCKS):
         pair_copy(step, plane_of(step)).wait_send()
         many(64, pair2_send.at[step], pair2_recv.at[step]).wait_send()

time: 63.5 us -> 62.3 us (0.981)
  Pallas kernels: 61.3 us -> 60.1 us
    pallas_call x1, Pallas kernels: 61.3 us -> 60.1 us  [body(): pl.pallas_call(kernel, out_shape=jax.ShapeDtypeStruct((ROWS, 256, C), BF1...]
where the time goes in v4:
time: 62.3 us; the launch traced here: 62.2 us
  Pallas kernels  60.1 us (96%)
  local copies, waits for them, and re-layouts  2.02 us (3%)
    pallas_call x1, Pallas kernels, body(): pl.pallas_call(kernel, out_shape=jax.ShapeDtypeStruct((ROWS, 256, C), BF1...  60.1 us
    transpose x1, local copies, waits for them, and re-layouts, body(): landed.reshape(ROWS, ROWS_HERE, OWN, C).transpose(1, 0, 2, 3)  2.02 us

profile of v4, /device:TPU:9, one launch (start us, length us, event | category | flops | bytes accessed | tf_op | source)
XLA Modules:
  0.0 62.2 jit_solution(14842965577809309707)
XLA Ops:
  0.0 60.1 %triangle.1 = bf16[8,256,128]{2,1,0:T(8,128)(2,1)} custom-call(bf16[64,32,128]{2,1,0:T(8,128)(2,1)} %pair_in.1, bf16[1,128]{1,0:T(2,128)(2,1)} %bitcast.11, bf16[128,512]{1,0:T(8,128)(2,1)} %proj_one_in.1, bf16[4,128]{1,0:T(4,128)(2,1)} %bitcast.9, bf16[128,128]{1,0:T(8,128)(2,1)} %out_one_in.1, bf16[1,128]{1,0:T(2,128)(2,1)} %bitcast.12, ...), custom_call_target="tpu_custom_call" | custom-call | tf_op jit(solution)/shard_map/triangle/pallas_call | solution.py:408
  60.2 2.0 %copy.10 = bf16[64,8,4,128]{3,2,1,0:T(4,128)(2,1)} copy(bf16[64,8,4,128]{3,2,0,1:T(4,128)(2,1)} %bitcast.8) | data formatting | bytes 1048576 | tf_op jit(solution)/shard_map/transpose | solution.py:455

commit v5 on v4

--- a/solution.py
+++ b/solution.py
@@ -342,8 +342,9 @@
 
     for line in range(OWN):
         line_parts(line, flat_f[pl.ds(line, N, OWN), :], gain_two, proj_two_ref, proj_two_t)
-    for step in (2, 3):
-        to_other_core(step)
+        if line == 1:
+            to_other_core(2)
+    to_other_core(3)
     for step in range(BLOCKS):
         pair2_copy(step).wait_recv()
 

time: 62.3 us -> 62.3 us (level)
  no operation moved by 1% of the time
where the time goes in v5:
time: 62.3 us; the launch traced here: 62.2 us
  Pallas kernels  60.1 us (96%)
  local copies, waits for them, and re-layouts  2.02 us (3%)
    pallas_call x1, Pallas kernels, body(): pl.pallas_call(kernel, out_shape=jax.ShapeDtypeStruct((ROWS, 256, C), BF1...  60.1 us
    transpose x1, local copies, waits for them, and re-layouts, body(): landed.reshape(ROWS, ROWS_HERE, OWN, C).transpose(1, 0, 2, 3)  2.02 us

profile of v5, /device:TPU:9, one launch (start us, length us, event | category | flops | bytes accessed | tf_op | source)
XLA Modules:
  0.0 62.2 jit_solution(16814726896926808276)
XLA Ops:
  0.0 60.1 %triangle.1 = bf16[8,256,128]{2,1,0:T(8,128)(2,1)} custom-call(bf16[64,32,128]{2,1,0:T(8,128)(2,1)} %pair_in.1, bf16[1,128]{1,0:T(2,128)(2,1)} %bitcast.11, bf16[128,512]{1,0:T(8,128)(2,1)} %proj_one_in.1, bf16[4,128]{1,0:T(4,128)(2,1)} %bitcast.9, bf16[128,128]{1,0:T(8,128)(2,1)} %out_one_in.1, bf16[1,128]{1,0:T(2,128)(2,1)} %bitcast.12, ...), custom_call_target="tpu_custom_call" | custom-call | tf_op jit(solution)/shard_map/triangle/pallas_call | solution.py:409
  60.2 2.0 %copy.10 = bf16[64,8,4,128]{3,2,1,0:T(4,128)(2,1)} copy(bf16[64,8,4,128]{3,2,0,1:T(4,128)(2,1)} %bitcast.8) | data formatting | bytes 1048576 | tf_op jit(solution)/shard_map/transpose | solution.py:456
